TPU v7x, 32 devices: a whole 2x2x4 slice. The times are simulated.
32 devices in a mesh: scen: 4 (over y, x), slab: 8 (over z, core).
Axes of the slice: x: 2, y: 2, z: 4, core: 2. Of those that a mesh axis runs over, the one named last changes fastest.
Arguments:
- start: float32 [4, 64, 256, 256], P('scen', 'slab'), may hold values from 0 to 2
- flow_east: float32 [4, 64, 256, 256], P('scen', 'slab'), may hold values from 0.3 to 1.2
- flow_north: float32 [4, 64, 256, 256], P('scen', 'slab'), may hold values from 0.3 to 1.2
- wells: int32 [64, 256, 256], P('slab'), may hold values 0 or 1
- monitors: int32 [64, 256, 256], P('slab'), may hold values 0 or 1
- control: float32 [4, 16, 4096], P('scen', 'slab'), may hold values from -3 to 3
- multiplier: float32 [4, 16, 4096], P('scen', 'slab'), may hold values from -3 to 3
- threshold: float32 [1], replicated, may hold values from 0.8 to 1.3
Outputs:
- final_fields: float32 [4, 64, 256, 256], P('scen', 'slab')
- consensus_next: float32 [16, 4096], P('slab')
- multiplier_next: float32 [4, 16, 4096], P('scen', 'slab')
- cvar: float32 [1], replicated
All inputs are finite; a program needn't handle non-finite values. No bound on the sum of `wells` or of `monitors` on one device may be relied on, other than what follows from the above.
Results may differ from a plain program's by a relative error of at most 0.00002.
Values sent between devices are 32-bit elements; how exact they have to be, the bound alone decides.
A program may use at most 192 MiB of HBM per device.

v0:
```python
import jax
import jax.numpy as jnp
from jax import lax
from jax.sharding import PartitionSpec as P

STEPS = 4


EPS_LIMIT = 0.01
TIME_STEP = 0.25
DIFF_FLAT = 0.1
DIFF_VERTICAL = 0.25
BETA_LEVEL = 0.75
SOFT_WIDTH = 0.25


def with_halo(cells, sides, width):
    for axis, dim in sides:
        count = lax.axis_size(axis)
        ends = count - 1
        head = lax.slice_in_dim(cells, 0, width, axis=dim)
        tail = lax.slice_in_dim(cells, cells.shape[dim] - width, cells.shape[dim], axis=dim)
        cells = jnp.concatenate(
            [
                lax.ppermute(tail, axis, [(i, (i + 1) % count) for i in range(ends)]),
                cells,
                lax.ppermute(head, axis, [((i + 1) % count, i) for i in range(ends)]),
            ],
            axis=dim,
        )
    return cells


def pad_axis(field, which_axis, low_pad, high_pad):
    widths = [(0, 0)] * field.ndim
    widths[which_axis] = (low_pad, high_pad)
    return jnp.pad(field, widths)


def second_difference(padded, field, which_axis):
    length = field.shape[which_axis]
    upper_cells = lax.slice_in_dim(padded, 2, length + 2, axis=which_axis)
    lower_cells = lax.slice_in_dim(padded, 0, length, axis=which_axis)
    return upper_cells - 2.0 * field + lower_cells


def divergence(field, velocity, which_axis):
    length = field.shape[which_axis]
    padded = pad_axis(field, which_axis, 1, 1)
    lower_cells = lax.slice_in_dim(padded, 0, length, axis=which_axis)
    upper_cells = lax.slice_in_dim(padded, 2, length + 2, axis=which_axis)
    backward = field - lower_cells
    forward = upper_cells - field
    product = backward * forward
    weight = (product + jnp.sqrt(product * product + EPS_LIMIT * EPS_LIMIT)) / (
        backward * backward + forward * forward + EPS_LIMIT
    )
    face_value = field + 0.5 * weight * (backward / 3.0 + 2.0 * forward / 3.0)
    fluxes = velocity * face_value
    previous = lax.slice_in_dim(pad_axis(fluxes, which_axis, 1, 0), 0, length, axis=which_axis)
    return fluxes - previous


def horizontal(field, flow_east, flow_north, rate):
    advect = divergence(field, flow_east, 1) + divergence(field, flow_north, 2)
    spread = second_difference(pad_axis(field, 1, 1, 1), field, 1) + second_difference(
        pad_axis(field, 2, 1, 1), field, 2
    )
    return -advect + DIFF_FLAT * spread - rate * field


def prolong(coarse, row_count, column_count):
    plane_count = coarse.shape[0]
    cube = coarse.reshape(plane_count, 1, row_count // 4, 1, column_count // 4, 1)
    cube = jnp.broadcast_to(cube, (plane_count, 4, row_count // 4, 4, column_count // 4, 4))
    return cube.reshape(plane_count * 4, row_count, column_count)


def restrict(fine):
    plane_count, row_count, column_count = fine.shape
    blocks = fine.reshape(plane_count // 4, 4, row_count // 4, 4, column_count // 4, 4).sum(
        axis=(1, 3, 5)
    )
    return blocks.reshape(plane_count // 4, row_count // 4 * (column_count // 4))


def on_device(start, flow_east, flow_north, wells, monitors, control, multiplier, threshold):
    scen_count = lax.axis_size("scen")
    slab_count = lax.axis_size("slab")
    consensus = lax.psum(jnp.sum(control + multiplier, axis=0), "scen") / scen_count
    field = start[0]
    east = flow_east[0]
    north = flow_north[0]
    plane_count, row_count, column_count = field.shape
    wells_float = wells.astype(jnp.float32)
    monitor_float = monitors.astype(jnp.float32)
    rate = wells_float * prolong(consensus, row_count, column_count)
    states = []
    for step_index in range(STEPS):
        states.append(field)
        padded = with_halo(field, (("slab", 0),), 1)
        vertical = second_difference(padded, field, 0)
        field = field + TIME_STEP * (
            horizontal(field, east, north, rate) + DIFF_VERTICAL * vertical
        )
    mass, count = lax.psum((jnp.sum(monitor_float * field * field), jnp.sum(monitor_float)), "slab")
    count = jnp.maximum(count, 1.0)
    loss = mass / count
    scaled = (loss - threshold[0]) / SOFT_WIDTH
    weight = jax.nn.sigmoid(scaled) / ((1.0 - BETA_LEVEL) * scen_count)
    soft_term = SOFT_WIDTH * jax.nn.softplus(scaled) / ((1.0 - BETA_LEVEL) * scen_count)
    risk = lax.psum(soft_term, "scen")
    adjoint = weight * 2.0 * monitor_float * field / count
    rate_grad = jnp.zeros_like(field)
    for step_index in reversed(range(STEPS)):
        state = states[step_index]
        padded = with_halo(adjoint, (("slab", 0),), 1)
        unused, pullback = jax.vjp(lambda values: horizontal(values, east, north, rate), state)
        (pulled,) = pullback(adjoint)
        rate_grad = rate_grad - TIME_STEP * state * adjoint
        vertical = second_difference(padded, adjoint, 0)
        adjoint = adjoint + TIME_STEP * (pulled + DIFF_VERTICAL * vertical)
    coarse_cells = plane_count * slab_count * row_count * column_count / 64.0
    gradient = coarse_cells * restrict(wells_float * rate_grad)
    total = lax.psum(gradient, "scen")
    consensus_next = consensus - total
    multiplier_next = multiplier + control - consensus_next[None]
    cvar = threshold + risk
    return (field[None], consensus_next, multiplier_next, cvar)


def solution(mesh):
    placed = (
        P("scen", "slab", None, None),
        P("scen", "slab", None, None),
        P("scen", "slab", None, None),
        P("slab", None, None),
        P("slab", None, None),
        P("scen", "slab", None),
        P("scen", "slab", None),
        P(),
    )
    return jax.shard_map(
        on_device,
        mesh=mesh,
        in_specs=placed,
        out_specs=(P("scen", "slab", None, None), P("slab", None), P("scen", "slab", None), P()),
        check_vma=False,
    )
```

profile of v0, /device:TPU:0, one launch (start us, length us, event | category | flops | bytes accessed | tf_op | source)
XLA Modules:
  0.0 423.0 jit_solution(2808476160678709573)
XLA Ops:
  3.0 3.0 collective-permute-start.1
  6.9 17.7 %psum.35 = f32[2,4096]{1,0:T(2,128)S(1)} all-reduce(f32[2,4096]{1,0:T(2,128)S(1)} %bitcast.40), channel_id=1, replica_groups=mesh['scen'=4,'slab'=8] {'scen'}, use_global_device_ids=true, to_apply=%region_0.0 | all-reduce | flops 8192 | bytes 65536 | tf_op jit(solution)/shard_map/psum | solution.py:90
  24.6 11.3 %bitcast_multiply_fusion.3 = (f32[8,256,256]{2,1,0:T(8,128)}, f32[8,256,256]{2,1,0:T(8,128)}) fusion(f32[1,8,256,256]{3,2,1,0:T(8,128)} %param.10, f32[8,256,256]{2,1,0:T(8,128)} %bitcast.37, f32[1,8,256,256]{3,2,1,0:T(8,128)} %param.9), kind=kLoop, calls=%fused_computation.197 | loop fusion | flops 18874368 | bytes 10485760 | tf_op jit(solution)/shard_map/mul | solution.py:59
  36.1 21.5 %broadcast_in_dim.17 = f32[2,4,64,4,64,4]{5,4,3,2,1,0:T(8,128)} broadcast(f32[2,64,64]{2,1,0:T(8,128)S(1)} %broadcast_in_dim.16), dimensions={0,2,4} | broadcast | bytes 2129920 | tf_op jit(solution)/shard_map/broadcast_in_dim | solution.py:75
  57.6 56.1 %reshape.22 = f32[8,256,256]{2,1,0:T(8,128)} reshape(f32[2,4,64,4,64,4]{5,4,3,2,1,0:T(8,128)} %broadcast_in_dim.17) | data formatting | bytes 4194304 | tf_op jit(solution)/shard_map/reshape | solution.py:76
  114.4 12.0 %fusion.7 = (f32[8,256,256]{2,1,0:T(8,128)S(1)}, f32[8,256,256]{2,1,0:T(8,128)S(1)}) fusion(f32[8,256,256]{2,1,0:T(8,128)} %bitcast.38, f32[8,256,256]{2,1,0:T(8,128)} %get-tuple-element.78, f32[8,256,256]{2,1,0:T(8,128)} %get-tuple-element.77, f32[1,256,256]{2,1,0:T(8,128)S(1)} %collective-permute-done.1, f32[1,256,256]{2,1,0:T(8,128)S(1)} %collective-permute-done, ...), kind=kLoop, calls=%fused_computation.48 | loop fusion | flops 12582912 | bytes 15204352 | tf_op jit(solution)/shard_map/add | solution.py:103
  127.7 3.0 collective-permute-start.3
  130.8 4.1 bitcast_multiply_fusion.2
  135.0 3.2 fusion.15
  139.5 4.2 %collective-permute-start.5 = (f32[1,256,256]{2,1,0:T(8,128)S(1)}, f32[1,256,256]{2,1,0:T(8,128)S(1)}, u32[]{:S(2)}, u32[]{:S(2)}) collective-permute-start(f32[1,256,256]{2,1,0:T(8,128)S(1)} %get-tuple-element.68), channel_id=1, source_target_pairs={{0,1},{1,2},{2,3},{3,4},{4,5},{5,6},{6,7},{8,9},{9,10},{10,11},{11... | collective-permute-start | bytes 786440 | tf_op jit(solution)/shard_map/ppermute | solution.py:25
  143.8 4.1 bitcast_multiply_fusion.1
  147.9 3.1 fusion.23
  152.4 4.4 %collective-permute-start.7 = (f32[1,256,256]{2,1,0:T(8,128)S(1)}, f32[1,256,256]{2,1,0:T(8,128)S(1)}, u32[]{:S(2)}, u32[]{:S(2)}) collective-permute-start(f32[1,256,256]{2,1,0:T(8,128)S(1)} %get-tuple-element.66), channel_id=1, source_target_pairs={{0,1},{1,2},{2,3},{3,4},{4,5},{5,6},{6,7},{8,9},{9,10},{10,11},{11... | collective-permute-start | bytes 786440 | tf_op jit(solution)/shard_map/ppermute | solution.py:25
  156.8 4.1 bitcast_multiply_fusion.4
  161.0 5.0 %fusion.42 = (f32[]{:T(128)}, f32[]{:T(128)}, f32[8,256,256]{2,1,0:T(8,128)}) fusion(s32[8,256,256]{2,1,0:T(8,128)S(1)} %copy-done.21, f32[8,256,256]{2,1,0:T(8,128)S(1)} %fusion.23, f32[1,256,256]{2,1,0:T(8,128)S(1)} %collective-permute-done.7, f32[1,256,256]{2,1,0:T(8,128)S(1)} %collective-permute-done.6, f32[8,256,256]{2,1,0:T(8,128)S(1)} %get-tuple-element.44, ...), kind=kLoop, calls=%fused_computation.83 | loop fusion | flops 14155774 | bytes 13107208 | tf_op jit(solution)/shard_map/reduce_sum | solution.py:106
  166.0 16.8 %all-reduce.46 = (f32[]{:T(128)}, f32[]{:T(128)}) all-reduce(f32[]{:T(128)} %get-tuple-element.5, f32[]{:T(128)} %get-tuple-element.4), channel_id=1, replica_groups=mesh['scen'=4,'slab'=8] {'slab'}, use_global_device_ids=true, to_apply=%region_4.5 | all-reduce | flops 2 | bytes 16 | tf_op jit(solution)/shard_map/psum | solution.py:106
  184.1 4.4 %broadcast_multiply_fusion.2 = (f32[8,256,256]{2,1,0:T(8,128)}, f32[8,256,256]{2,1,0:T(8,128)S(1)}) fusion(f32[]{:T(128)S(6)} %max.7, f32[8,256,256]{2,1,0:T(8,128)} %get-tuple-element.42, s32[8,256,256]{2,1,0:T(8,128)} %param.12, f32[]{:T(128)S(6)} %mul.747), kind=kLoop, calls=%fused_computation.295 | loop fusion | flops 2621440 | bytes 8388616 | tf_op jit(solution)/shard_map/transpose(jvp())/mul | solution.py:69
  188.5 8.3 %fusion.45 = (f32[8,256,256]{2,1,0:T(8,128)}, f32[8,256,256]{2,1,0:T(8,128)S(1)}, f32[8,256,256]{2,1,0:T(8,128)}, f32[8,256,256]{2,1,0:T(8,128)S(1)}) fusion(f32[8,256,256]{2,1,0:T(8,128)S(1)} %copy-done.10, f32[8,256,256]{2,1,0:T(8,128)S(1)} %get-tuple-element.33, f32[1,8,256,256]{3,2,1,0:T(8,128)S(1)} %copy-done, f32[1,8,256,256]{3,2,1,0:T(8,128)S(1)} %copy-done.2), kind=kLoop, calls=%fused_computation.86 | loop fusion | flops 39321600 | bytes 16777216 | tf_op jit(solution)/shard_map/transpose(jvp())/add_any | solution.py:54
  198.1 3.2 collective-permute-start.9
  201.4 8.5 %fusion.190 = (f32[8,256,256]{2,1,0:T(8,128)}, f32[8,256,256]{2,1,0:T(8,128)}, f32[8,256,256]{2,1,0:T(8,128)}, f32[8,256,256]{2,1,0:T(8,128)}) fusion(f32[8,256,256]{2,1,0:T(8,128)S(1)} %get-tuple-element.35, f32[8,256,256]{2,1,0:T(8,128)S(1)} %copy-done.10, f32[8,256,256]{2,1,0:T(8,128)S(1)} %get-tuple-element.50), kind=kLoop, calls=%fused_computation.312 | loop fusion | flops 37748736 | bytes 14680064 | tf_op jit(solution)/shard_map/transpose(jvp())/neg | solution.py:52
  210.0 16.8 %broadcast_multiply_fusion.1 = (f32[8,256,256]{2,1,0:T(8,128)}, f32[8,256,256]{2,1,0:T(8,128)S(1)}) fusion(f32[8,256,256]{2,1,0:T(8,128)} %copy-done.13, f32[1,256,256]{2,1,0:T(8,128)S(1)} %collective-permute-done.9, f32[1,256,256]{2,1,0:T(8,128)S(1)} %collective-permute-done.8, f32[8,256,256]{2,1,0:T(8,128)} %get-tuple-element.59, ...), kind=kLoop, calls=%fused_computation.294 | loop fusion | flops 16777216 | bytes 27787264 | tf_op jit(solution)/shard_map/transpose(jvp())/mul | solution.py:69
  226.8 8.3 %fusion.51 = (f32[8,256,256]{2,1,0:T(8,128)}, f32[8,256,256]{2,1,0:T(8,128)S(1)}, f32[8,256,256]{2,1,0:T(8,128)}, f32[8,256,256]{2,1,0:T(8,128)S(1)}) fusion(f32[8,256,256]{2,1,0:T(8,128)S(1)} %copy-done.8, f32[8,256,256]{2,1,0:T(8,128)S(1)} %get-tuple-element.23, f32[1,8,256,256]{3,2,1,0:T(8,128)S(1)} %copy-done, f32[1,8,256,256]{3,2,1,0:T(8,128)S(1)} %copy-done.3), kind=kLoop, calls=%fused_computation.92 | loop fusion | flops 39321600 | bytes 16777216 | tf_op jit(solution)/shard_map/transpose(jvp())/add_any | solution.py:54
  236.5 3.3 collective-permute-start.11
  239.8 8.4 %fusion.184 = (f32[8,256,256]{2,1,0:T(8,128)}, f32[8,256,256]{2,1,0:T(8,128)}, f32[8,256,256]{2,1,0:T(8,128)}, f32[8,256,256]{2,1,0:T(8,128)}) fusion(f32[8,256,256]{2,1,0:T(8,128)S(1)} %get-tuple-element.25, f32[8,256,256]{2,1,0:T(8,128)S(1)} %copy-done.8, f32[8,256,256]{2,1,0:T(8,128)S(1)} %get-tuple-element.48), kind=kLoop, calls=%fused_computation.310 | loop fusion | flops 37748736 | bytes 14680064 | tf_op jit(solution)/shard_map/transpose(jvp())/neg | solution.py:52
  248.3 16.4 %broadcast_multiply_fusion = (f32[8,256,256]{2,1,0:T(8,128)}, f32[8,256,256]{2,1,0:T(8,128)}) fusion(f32[8,256,256]{2,1,0:T(8,128)} %copy-done.14, f32[1,256,256]{2,1,0:T(8,128)S(1)} %collective-permute-done.11, f32[1,256,256]{2,1,0:T(8,128)S(1)} %collective-permute-done.10, f32[8,256,256]{2,1,0:T(8,128)} %get-tuple-element.55, ...), kind=kLoop, calls=%fused_computation.293 | loop fusion | flops 16777216 | bytes 27787264 | tf_op jit(solution)/shard_map/transpose(jvp())/mul | solution.py:69
  264.7 10.2 %fusion.57 = (f32[8,256,256]{2,1,0:T(8,128)}, f32[8,256,256]{2,1,0:T(8,128)S(1)}, f32[8,256,256]{2,1,0:T(8,128)}, f32[8,256,256]{2,1,0:T(8,128)S(1)}) fusion(f32[8,256,256]{2,1,0:T(8,128)S(1)} %copy-done.12, f32[8,256,256]{2,1,0:T(8,128)} %get-tuple-element.13, f32[1,8,256,256]{3,2,1,0:T(8,128)S(1)} %copy-done, f32[1,8,256,256]{3,2,1,0:T(8,128)S(1)} %copy-done.3), kind=kLoop, calls=%fused_computation.98 | loop fusion | flops 39321600 | bytes 16777216 | tf_op jit(solution)/shard_map/transpose(jvp())/add_any | solution.py:54
  277.6 4.5 %collective-permute-start.13 = (f32[1,256,256]{2,1,0:T(8,128)S(1)}, f32[1,256,256]{2,1,0:T(8,128)S(1)}, u32[]{:S(2)}, u32[]{:S(2)}) collective-permute-start(f32[1,256,256]{2,1,0:T(8,128)S(1)} %get-tuple-element.54), channel_id=1, source_target_pairs={{0,1},{1,2},{2,3},{3,4},{4,5},{5,6},{6,7},{8,9},{9,10},{10,11},{11... | collective-permute-start | bytes 786440 | tf_op jit(solution)/shard_map/ppermute | solution.py:25
  282.1 8.5 %fusion.177 = (f32[8,256,256]{2,1,0:T(8,128)}, f32[8,256,256]{2,1,0:T(8,128)}, f32[8,256,256]{2,1,0:T(8,128)}, f32[8,256,256]{2,1,0:T(8,128)}) fusion(f32[8,256,256]{2,1,0:T(8,128)S(1)} %get-tuple-element.15, f32[8,256,256]{2,1,0:T(8,128)S(1)} %copy-done.12, f32[8,256,256]{2,1,0:T(8,128)S(1)} %get-tuple-element.46), kind=kLoop, calls=%fused_computation.308 | loop fusion | flops 37748736 | bytes 14680064 | tf_op jit(solution)/shard_map/transpose(jvp())/neg | solution.py:52
  290.6 21.2 %fusion.68 = f32[8,256,256]{2,1,0:T(8,128)} fusion(f32[8,256,256]{2,1,0:T(8,128)} %get-tuple-element.13, f32[1,256,256]{2,1,0:T(8,128)S(1)} %collective-permute-done.13, f32[1,256,256]{2,1,0:T(8,128)S(1)} %collective-permute-done.12, f32[8,256,256]{2,1,0:T(8,128)} %get-tuple-element.51, f32[8,256,256]{2,1,0:T(8,128)} %get-tuple-element.45, ...), kind=kLoop, calls=%fused_computation.110 | loop fusion | flops 23592960 | bytes 40370176 | tf_op jit(solution)/shard_map/mul | solution.py:124
  311.8 71.4 %reshape.23 = f32[2,4,64,4,64,4]{5,4,3,2,1,0:T(8,128)} reshape(f32[8,256,256]{2,1,0:T(8,128)} %fusion.68) | data formatting | bytes 4194304 | tf_op jit(solution)/shard_map/reshape | solution.py:81
  383.3 20.8 %reduce_sum.36 = f32[2,64,64]{2,1,0:T(8,128)S(1)} reduce(f32[2,4,64,4,64,4]{5,4,3,2,1,0:T(8,128)} %reshape.23, f32[]{:T(128)} %constant.79.clone.1), dimensions={1,3,5}, to_apply=%region_5.6 | reduce | flops 516096 | bytes 2129924 | tf_op jit(solution)/shard_map/reduce_sum | solution.py:81
  404.2 16.1 %all-reduce.47 = (f32[2,4096]{1,0:T(2,128)S(1)}, f32[1]{0:T(128)}) all-reduce(f32[2,4096]{1,0:T(2,128)S(1)} %mul.863, f32[1]{0:T(128)} %bitcast.9), channel_id=1, replica_groups=mesh['scen'=4,'slab'=8] {'scen'}, use_global_device_ids=true, to_apply=%region_6.7 | all-reduce | flops 8193 | bytes 65544 | tf_op jit(solution)/shard_map/psum | solution.py:125
  (86 shorter events, 13.6 us)
Async XLA Ops:
  1.7 112.6 %collective-permute-start = (f32[1,256,256]{2,1,0:T(8,128)S(1)}, f32[1,256,256]{2,1,0:T(8,128)S(1)}, u32[]{:S(2)}, u32[]{:S(2)}) collective-permute-start(f32[1,256,256]{2,1,0:T(8,128)S(1)} %get-tuple-element.75), channel_id=1, source_target_pairs={{1,0},{2,1},{3,2},{4,3},{5,4},{6,5},{7,6},{9,8},{10,9},{11,10},{12... | collective-permute-start | bytes 786440 | tf_op jit(solution)/shard_map/ppermute | solution.py:27
  3.0 111.3 %collective-permute-start.1 = (f32[1,256,256]{2,1,0:T(8,128)S(1)}, f32[1,256,256]{2,1,0:T(8,128)S(1)}, u32[]{:S(2)}, u32[]{:S(2)}) collective-permute-start(f32[1,256,256]{2,1,0:T(8,128)S(1)} %get-tuple-element.76), channel_id=1, source_target_pairs={{0,1},{1,2},{2,3},{3,4},{4,5},{5,6},{6,7},{8,9},{9,10},{10,11},{11... | collective-permute-start | bytes 786440 | tf_op jit(solution)/shard_map/ppermute | solution.py:25
  6.9 29.1 %copy-start.22 = (f32[1,2,4096]{2,1,0:T(2,128)}, f32[1,2,4096]{2,1,0:T(2,128)S(1)}, u32[]{:S(2)}) copy-start(f32[1,2,4096]{2,1,0:T(2,128)S(1)} %add.433) | copy-start | bytes 98308
  24.6 11.4 %copy-start.24 = (f32[2,4096]{1,0:T(2,128)}, f32[2,4096]{1,0:T(2,128)S(1)}, u32[]{:S(2)}) copy-start(f32[2,4096]{1,0:T(2,128)S(1)} %psum.35) | copy-start | bytes 98308
  114.3 16.5 %copy-start = (f32[1,8,256,256]{3,2,1,0:T(8,128)S(1)}, f32[1,8,256,256]{3,2,1,0:T(8,128)}, u32[]{:S(2)}) copy-start(f32[1,8,256,256]{3,2,1,0:T(8,128)} %param.10) | copy-start | bytes 6291460
  114.3 16.5 %copy-start.1 = (f32[1,8,256,256]{3,2,1,0:T(8,128)S(1)}, f32[1,8,256,256]{3,2,1,0:T(8,128)}, u32[]{:S(2)}) copy-start(f32[1,8,256,256]{3,2,1,0:T(8,128)} %param.9) | copy-start | bytes 6291460
  126.4 8.6 %copy-start.11 = (f32[8,256,256]{2,1,0:T(8,128)}, f32[8,256,256]{2,1,0:T(8,128)S(1)}, u32[]{:S(2)}) copy-start(f32[8,256,256]{2,1,0:T(8,128)S(1)} %get-tuple-element.43) | copy-start | bytes 6291460
  126.4 34.6 %copy-start.4 = (f32[8,256,256]{2,1,0:T(8,128)}, f32[8,256,256]{2,1,0:T(8,128)S(1)}, u32[]{:S(2)}) copy-start(f32[8,256,256]{2,1,0:T(8,128)S(1)} %get-tuple-element.44) | copy-start | bytes 6291460
  126.4 8.5 %collective-permute-start.2 = (f32[1,256,256]{2,1,0:T(8,128)S(1)}, f32[1,256,256]{2,1,0:T(8,128)S(1)}, u32[]{:S(2)}, u32[]{:S(2)}) collective-permute-start(f32[1,256,256]{2,1,0:T(8,128)S(1)} %get-tuple-element.71), channel_id=1, source_target_pairs={{1,0},{2,1},{3,2},{4,3},{5,4},{6,5},{7,6},{9,8},{10,9},{11,10},{12... | collective-permute-start | bytes 786440 | tf_op jit(solution)/shard_map/ppermute | solution.py:27
  127.7 7.2 %collective-permute-start.3 = (f32[1,256,256]{2,1,0:T(8,128)S(1)}, f32[1,256,256]{2,1,0:T(8,128)S(1)}, u32[]{:S(2)}, u32[]{:S(2)}) collective-permute-start(f32[1,256,256]{2,1,0:T(8,128)S(1)} %get-tuple-element.72), channel_id=1, source_target_pairs={{0,1},{1,2},{2,3},{3,4},{4,5},{5,6},{6,7},{8,9},{9,10},{10,11},{11... | collective-permute-start | bytes 786440 | tf_op jit(solution)/shard_map/ppermute | solution.py:25
  138.1 9.8 %copy-start.7 = (f32[8,256,256]{2,1,0:T(8,128)}, f32[8,256,256]{2,1,0:T(8,128)S(1)}, u32[]{:S(2)}) copy-start(f32[8,256,256]{2,1,0:T(8,128)S(1)} %fusion.15) | copy-start | bytes 6291460
  138.2 9.7 %collective-permute-start.4 = (f32[1,256,256]{2,1,0:T(8,128)S(1)}, f32[1,256,256]{2,1,0:T(8,128)S(1)}, u32[]{:S(2)}, u32[]{:S(2)}) collective-permute-start(f32[1,256,256]{2,1,0:T(8,128)S(1)} %get-tuple-element.67), channel_id=1, source_target_pairs={{1,0},{2,1},{3,2},{4,3},{5,4},{6,5},{7,6},{9,8},{10,9},{11,10},{12... | collective-permute-start | bytes 786440 | tf_op jit(solution)/shard_map/ppermute | solution.py:27
  139.5 8.4 %collective-permute-start.5 = (f32[1,256,256]{2,1,0:T(8,128)S(1)}, f32[1,256,256]{2,1,0:T(8,128)S(1)}, u32[]{:S(2)}, u32[]{:S(2)}) collective-permute-start(f32[1,256,256]{2,1,0:T(8,128)S(1)} %get-tuple-element.68), channel_id=1, source_target_pairs={{0,1},{1,2},{2,3},{3,4},{4,5},{5,6},{6,7},{8,9},{9,10},{10,11},{11... | collective-permute-start | bytes 786440 | tf_op jit(solution)/shard_map/ppermute | solution.py:25
  151.0 9.9 %copy-start.9 = (f32[8,256,256]{2,1,0:T(8,128)}, f32[8,256,256]{2,1,0:T(8,128)S(1)}, u32[]{:S(2)}) copy-start(f32[8,256,256]{2,1,0:T(8,128)S(1)} %fusion.23) | copy-start | bytes 6291460
  151.1 9.9 %collective-permute-start.6 = (f32[1,256,256]{2,1,0:T(8,128)S(1)}, f32[1,256,256]{2,1,0:T(8,128)S(1)}, u32[]{:S(2)}, u32[]{:S(2)}) collective-permute-start(f32[1,256,256]{2,1,0:T(8,128)S(1)} %get-tuple-element.65), channel_id=1, source_target_pairs={{1,0},{2,1},{3,2},{4,3},{5,4},{6,5},{7,6},{9,8},{10,9},{11,10},{12... | collective-permute-start | bytes 786440 | tf_op jit(solution)/shard_map/ppermute | solution.py:27
  152.4 8.6 %copy-start.21 = (s32[8,256,256]{2,1,0:T(8,128)S(1)}, s32[8,256,256]{2,1,0:T(8,128)}, u32[]{:S(2)}) copy-start(s32[8,256,256]{2,1,0:T(8,128)} %param.12) | copy-start | bytes 6291460
  152.4 8.6 %collective-permute-start.7 = (f32[1,256,256]{2,1,0:T(8,128)S(1)}, f32[1,256,256]{2,1,0:T(8,128)S(1)}, u32[]{:S(2)}, u32[]{:S(2)}) collective-permute-start(f32[1,256,256]{2,1,0:T(8,128)S(1)} %get-tuple-element.66), channel_id=1, source_target_pairs={{0,1},{1,2},{2,3},{3,4},{4,5},{5,6},{6,7},{8,9},{9,10},{10,11},{11... | collective-permute-start | bytes 786440 | tf_op jit(solution)/shard_map/ppermute | solution.py:25
  196.8 13.2 %collective-permute-start.8 = (f32[1,256,256]{2,1,0:T(8,128)S(1)}, f32[1,256,256]{2,1,0:T(8,128)S(1)}, u32[]{:S(2)}, u32[]{:S(2)}) collective-permute-start(f32[1,256,256]{2,1,0:T(8,128)S(1)} %get-tuple-element.61), channel_id=1, source_target_pairs={{1,0},{2,1},{3,2},{4,3},{5,4},{6,5},{7,6},{9,8},{10,9},{11,10},{12... | collective-permute-start | bytes 786440 | tf_op jit(solution)/shard_map/ppermute | solution.py:27
  198.1 11.9 %collective-permute-start.9 = (f32[1,256,256]{2,1,0:T(8,128)S(1)}, f32[1,256,256]{2,1,0:T(8,128)S(1)}, u32[]{:S(2)}, u32[]{:S(2)}) collective-permute-start(f32[1,256,256]{2,1,0:T(8,128)S(1)} %get-tuple-element.62), channel_id=1, source_target_pairs={{0,1},{1,2},{2,3},{3,4},{4,5},{5,6},{6,7},{8,9},{9,10},{10,11},{11... | collective-permute-start | bytes 786440 | tf_op jit(solution)/shard_map/ppermute | solution.py:25
  210.0 16.8 %copy-start.3 = (f32[1,8,256,256]{3,2,1,0:T(8,128)S(1)}, f32[1,8,256,256]{3,2,1,0:T(8,128)}, u32[]{:S(2)}) copy-start(f32[1,8,256,256]{3,2,1,0:T(8,128)} %param.9) | copy-start | bytes 6291460
  210.0 16.8 %copy-start.8 = (f32[8,256,256]{2,1,0:T(8,128)S(1)}, f32[8,256,256]{2,1,0:T(8,128)}, u32[]{:S(2)}) copy-start(f32[8,256,256]{2,1,0:T(8,128)} %copy-done.7) | copy-start | bytes 6291460
  235.1 13.1 %copy-start.19 = (f32[8,256,256]{2,1,0:T(8,128)}, f32[8,256,256]{2,1,0:T(8,128)S(1)}, u32[]{:S(2)}) copy-start(f32[8,256,256]{2,1,0:T(8,128)S(1)} %get-tuple-element.25) | copy-start | bytes 6291460
  235.1 13.1 %copy-start.20 = (f32[8,256,256]{2,1,0:T(8,128)}, f32[8,256,256]{2,1,0:T(8,128)S(1)}, u32[]{:S(2)}) copy-start(f32[8,256,256]{2,1,0:T(8,128)S(1)} %get-tuple-element.48) | copy-start | bytes 6291460
  235.2 13.0 %collective-permute-start.10 = (f32[1,256,256]{2,1,0:T(8,128)S(1)}, f32[1,256,256]{2,1,0:T(8,128)S(1)}, u32[]{:S(2)}, u32[]{:S(2)}) collective-permute-start(f32[1,256,256]{2,1,0:T(8,128)S(1)} %get-tuple-element.57), channel_id=1, source_target_pairs={{1,0},{2,1},{3,2},{4,3},{5,4},{6,5},{7,6},{9,8},{10,9},{11,10},{12... | collective-permute-start | bytes 786440 | tf_op jit(solution)/shard_map/ppermute | solution.py:27
  236.5 11.7 %collective-permute-start.11 = (f32[1,256,256]{2,1,0:T(8,128)S(1)}, f32[1,256,256]{2,1,0:T(8,128)S(1)}, u32[]{:S(2)}, u32[]{:S(2)}) collective-permute-start(f32[1,256,256]{2,1,0:T(8,128)S(1)} %get-tuple-element.58), channel_id=1, source_target_pairs={{0,1},{1,2},{2,3},{3,4},{4,5},{5,6},{6,7},{8,9},{9,10},{10,11},{11... | collective-permute-start | bytes 786440 | tf_op jit(solution)/shard_map/ppermute | solution.py:25
  248.3 16.4 %copy-start.12 = (f32[8,256,256]{2,1,0:T(8,128)S(1)}, f32[8,256,256]{2,1,0:T(8,128)}, u32[]{:S(2)}) copy-start(f32[8,256,256]{2,1,0:T(8,128)} %copy-done.11) | copy-start | bytes 6291460
  274.8 15.7 %copy-start.15 = (f32[8,256,256]{2,1,0:T(8,128)}, f32[8,256,256]{2,1,0:T(8,128)S(1)}, u32[]{:S(2)}) copy-start(f32[8,256,256]{2,1,0:T(8,128)S(1)} %get-tuple-element.15) | copy-start | bytes 6291460
  274.8 15.7 %copy-start.16 = (f32[8,256,256]{2,1,0:T(8,128)}, f32[8,256,256]{2,1,0:T(8,128)S(1)}, u32[]{:S(2)}) copy-start(f32[8,256,256]{2,1,0:T(8,128)S(1)} %get-tuple-element.46) | copy-start | bytes 6291460
  276.3 14.3 %collective-permute-start.12 = (f32[1,256,256]{2,1,0:T(8,128)S(1)}, f32[1,256,256]{2,1,0:T(8,128)S(1)}, u32[]{:S(2)}, u32[]{:S(2)}) collective-permute-start(f32[1,256,256]{2,1,0:T(8,128)S(1)} %get-tuple-element.53), channel_id=1, source_target_pairs={{1,0},{2,1},{3,2},{4,3},{5,4},{6,5},{7,6},{9,8},{10,9},{11,10},{12... | collective-permute-start | bytes 786440 | tf_op jit(solution)/shard_map/ppermute | solution.py:27
  277.6 13.0 %collective-permute-start.13 = (f32[1,256,256]{2,1,0:T(8,128)S(1)}, f32[1,256,256]{2,1,0:T(8,128)S(1)}, u32[]{:S(2)}, u32[]{:S(2)}) collective-permute-start(f32[1,256,256]{2,1,0:T(8,128)S(1)} %get-tuple-element.54), channel_id=1, source_target_pairs={{0,1},{1,2},{2,3},{3,4},{4,5},{5,6},{6,7},{8,9},{9,10},{10,11},{11... | collective-permute-start | bytes 786440 | tf_op jit(solution)/shard_map/ppermute | solution.py:25
  383.3 37.0 %copy-start.23 = (f32[1,2,4096]{2,1,0:T(2,128)S(1)}, f32[1,2,4096]{2,1,0:T(2,128)}, u32[]{:S(2)}) copy-start(f32[1,2,4096]{2,1,0:T(2,128)} %copy-done.22) | copy-start | bytes 98308
  383.3 37.0 %copy-start.25 = (f32[2,4096]{1,0:T(2,128)S(1)}, f32[2,4096]{1,0:T(2,128)}, u32[]{:S(2)}) copy-start(f32[2,4096]{1,0:T(2,128)} %copy-done.24) | copy-start | bytes 98308
  (8 other events, 51.6 us)
where the time goes:
time: 431 us; the launch traced here: 423 us
  other arithmetic  180 us (42%)
  local copies, waits for them, and re-layouts  152 us (35%)
  blocking collectives  50.6 us (12%)
  starting transfers between devices  34.7 us (8%)
  between operations  5.42 us (1%)
    reshape x1, local copies, waits for them, and re-layouts, restrict(): fine.reshape(plane_count // 4, 4, row_count // 4, 4, column_count // 4, 4)  71.4 us
    reshape x1, local copies, waits for them, and re-layouts, prolong(): return cube.reshape(plane_count * 4, row_count, column_count)  56.1 us
    mul x3, other arithmetic, horizontal(): return -advect + DIFF_FLAT * spread - rate * field  37.5 us
    add_any x3, other arithmetic, divergence(): product = backward * forward  26.7 us
    ppermute x7, starting transfers between devices, with_halo(): lax.ppermute(tail, axis, [(i, (i + 1) % count) for i in range(ends)])  25.7 us
    neg x3, other arithmetic, divergence(): backward = field - lower_cells  25.5 us
    mul x4, other arithmetic, divergence(): fluxes = velocity * face_value  23.7 us
    broadcast_in_dim x2, local copies, waits for them, and re-layouts, prolong(): jnp.broadcast_to(cube, (plane_count, 4, row_count // 4, 4, column_count /...  21.6 us
  transfers between devices with their start and end apart: 14, of which 0 were waited for; matrix products, arithmetic and copies ran while one was open for 30% of the time, Pallas kernels for 0%

commit v1 on v0

v1 whole, which is shorter than its diff:
```python
import functools

import jax
import jax.numpy as jnp
from jax import lax
from jax.experimental import pallas as pl
from jax.experimental.pallas import tpu as pltpu
from jax.sharding import PartitionSpec as P

STEPS = 4
EPS_LIMIT = 0.01
TIME_STEP = 0.25
DIFF_FLAT = 0.1
DIFF_VERTICAL = 0.25
BETA_LEVEL = 0.75
SOFT_WIDTH = 0.25

LANES = 128
CELL = 4
CHUNKS = 4

DT_FLAT = TIME_STEP * DIFF_FLAT
DT_VERT = TIME_STEP * DIFF_VERTICAL
KEEP = 1.0 - 2.0 * DT_VERT
MESH = pl.DeviceIdType.MESH
HIGHEST = lax.Precision.HIGHEST


def limiter(a, b, q):
    p = a * b
    s2 = p * p + EPS_LIMIT * EPS_LIMIT
    rs = lax.rsqrt(s2)
    rq = pl.reciprocal(q, approx=True)
    return (p + s2 * rs) * rq, rs, rq


def slopes(a, b, t, rs, rq, uw):
    rq2 = rq + rq
    uwt = uw * t
    da = uw + uwt * (b * rs - a * rq2)
    db = (uw + uw - DT_FLAT) + uwt * (a * rs - b * rq2)
    return da, db


def kernel(
    scen_count,
    slab_count,
    start_hbm,
    east_hbm,
    north_hbm,
    wells_hbm,
    monitors_hbm,
    control,
    multiplier,
    threshold,
    fields_hbm,
    consensus_next,
    multiplier_next,
    cvar,
    state,
    lam,
    grad,
    ux,
    uy,
    wells,
    monitors,
    decay,
    coef,
    halo,
    spread_in,
    spread,
    gathered,
    cons,
    shares,
    sums,
    pulls,
    totals,
    load_sem,
    out_sem,
    halo_send,
    halo_recv,
    cons_send,
    cons_recv,
    sum_send,
    sum_recv,
    pull_send,
    pull_recv,
):
    planes, rows, cols = start_hbm.shape[1:]
    pieces = cols // LANES
    size = rows // CHUNKS
    per_lane = LANES // (cols // CELL)
    group = CELL * per_lane
    groups = size // group
    tiles = rows // group
    coarse_planes = planes // CELL
    scen = lax.axis_index("scen")
    slab = lax.axis_index("slab")
    last = slab_count - 1
    lane = lax.broadcasted_iota(jnp.int32, (planes, LANES), 1)
    level = lax.broadcasted_iota(jnp.int32, (planes, LANES), 0)
    lane_first = lane == 0
    lane_last = lane == LANES - 1
    level_first = level == 0
    level_last = level == planes - 1
    zero = jnp.zeros((planes, LANES), jnp.float32)

    def get(ref, *where):
        return [ref[(*where, slice(None), pl.ds(i * LANES, LANES))] for i in range(pieces)]

    def put(ref, values, *where):
        for i in range(pieces):
            ref[(*where, slice(None), pl.ds(i * LANES, LANES))] = values[i]

    def ahead(vs):
        nexts = vs[1:] + [zero]
        return [pltpu.roll(jnp.where(lane_first, n, v), LANES - 1, 1) for v, n in zip(vs, nexts)]

    def behind(vs, fill):
        out = [jnp.where(lane_first, fill, pltpu.roll(vs[0], 1, 1))]
        for v, n in zip(vs[1:], vs[:-1]):
            out.append(pltpu.roll(jnp.where(lane_last, n, v), 1, 1))
        return out

    def vertical(vs, hs):
        out = []
        for v, h in zip(vs, hs):
            below = jnp.where(level_first, h, pltpu.roll(v, 1, 0))
            above = jnp.where(level_last, h, pltpu.roll(v, planes - 1, 0))
            out.append(below + above)
        return out

    arrays = (
        (start_hbm.at[0], state.at[0]),
        (east_hbm.at[0], ux),
        (north_hbm.at[0], uy),
        (wells_hbm, wells),
        (monitors_hbm, monitors),
    )

    def load(which, chunk):
        source, target = arrays[which]
        span = pl.ds(chunk * size, size)
        for z in range(planes):
            pltpu.make_async_copy(
                source.at[z, span, :], target.at[span, z, :], load_sem.at[which, chunk]
            ).start()

    def loaded(which, chunk):
        target = arrays[which][1].at[pl.ds(chunk * size, size)]
        pltpu.make_async_copy(target, target, load_sem.at[which, chunk]).wait()

    def load_chunk(chunk, carry):
        for which in range(4):
            load(which, chunk)
        return carry

    lax.fori_loop(0, CHUNKS, load_chunk, 0)

    def load_monitors(chunk, carry):
        load(4, chunk)
        return carry

    lax.fori_loop(0, CHUNKS, load_monitors, 0)

    gathered[scen] = control[0] + multiplier[0]

    def clear(x, carry):
        for i in range(2):
            put(halo, [zero] * pieces, i, x)
        return carry

    lax.fori_loop(0, rows, clear, 0)
    for k in range(STEPS + 1):
        put(state, [zero] * pieces, k, rows)
    for i in range(2):
        put(lam, [zero] * pieces, i, rows)
        put(lam, [zero] * pieces, i, rows + 1)
    for k in range(STEPS - 1):
        put(coef, [zero] * pieces, k, 0, rows)

    barrier = pltpu.get_barrier_semaphore()
    for d in range(1, slab_count):
        pl.semaphore_signal(
            barrier, inc=1, device_id={"slab": lax.rem(slab + d, slab_count)}, device_id_type=MESH
        )
    for d in range(1, scen_count):
        pl.semaphore_signal(
            barrier, inc=1, device_id={"scen": lax.rem(scen + d, scen_count)}, device_id_type=MESH
        )

    pl.semaphore_wait(barrier, slab_count + scen_count - 2)

    def everyone(axis, me, count, buffer, send_sem, recv_sem):
        copies = []
        for d in range(1, count):
            copies.append(
                pltpu.make_async_remote_copy(
                    src_ref=buffer.at[me],
                    dst_ref=buffer.at[me],
                    send_sem=send_sem.at[d - 1],
                    recv_sem=recv_sem.at[d - 1],
                    device_id={axis: lax.rem(me + d, count)},
                    device_id_type=MESH,
                )
            )
        return copies

    cons_copies = everyone("scen", scen, scen_count, gathered, cons_send, cons_recv)
    for copy in cons_copies:
        copy.start()

    def rise(source, e, chunk):
        return pltpu.make_async_remote_copy(
            src_ref=source,
            dst_ref=halo.at[e % 2, pl.ds(chunk * size, size), 0, :],
            send_sem=halo_send.at[e, 0, chunk],
            recv_sem=halo_recv.at[e, 0, chunk],
            device_id={"slab": jnp.minimum(slab + 1, last)},
            device_id_type=MESH,
        )

    def sink(source, e, chunk):
        return pltpu.make_async_remote_copy(
            src_ref=source,
            dst_ref=halo.at[e % 2, pl.ds(chunk * size, size), planes - 1, :],
            send_sem=halo_send.at[e, 1, chunk],
            recv_sem=halo_recv.at[e, 1, chunk],
            device_id={"slab": jnp.maximum(slab - 1, 0)},
            device_id_type=MESH,
        )

    def plane(ref, chunk, z):
        return ref.at[pl.ds(chunk * size, size), z, :]

    def send(ref, e, chunk):
        @pl.when(slab < last)
        def _():
            rise(plane(ref, chunk, planes - 1), e, chunk).start()

        @pl.when(slab > 0)
        def _():
            sink(plane(ref, chunk, 0), e, chunk).start()

    def arrived(e, chunk):
        here = halo.at[e % 2]

        @pl.when(slab > 0)
        def _():
            rise(plane(here, chunk, 0), e, chunk).wait_recv()

        @pl.when(slab < last)
        def _():
            sink(plane(here, chunk, planes - 1), e, chunk).wait_recv()

    def sent(ref, e, chunk):
        @pl.when(slab < last)
        def _():
            rise(plane(ref, chunk, planes - 1), e, chunk).wait_send()

        @pl.when(slab > 0)
        def _():
            sink(plane(ref, chunk, 0), e, chunk).wait_send()

    def first_send(chunk, carry):
        span = pl.ds(chunk * size, size)

        @pl.when(slab < last)
        def _():
            rise(start_hbm.at[0, planes - 1, span, :], 0, chunk).start()

        @pl.when(slab > 0)
        def _():
            sink(start_hbm.at[0, 0, span, :], 0, chunk).start()

        return carry

    lax.fori_loop(0, CHUNKS, first_send, 0)

    for copy in cons_copies:
        copy.wait()
    total = gathered[0]
    for s in range(1, scen_count):
        total = total + gathered[s]
    cons[...] = total / scen_count
    for k in range(tiles):
        part = cons[:, pl.ds(k * LANES, LANES)]
        spread_in[pl.ds(k * planes, planes), :] = jnp.concatenate(
            [jnp.broadcast_to(part[p : p + 1], (CELL, LANES)) for p in range(coarse_planes)], axis=0
        )
    wide = per_lane * cols
    repeat = (
        lax.broadcasted_iota(jnp.int32, (LANES, wide), 0)
        == lax.broadcasted_iota(jnp.int32, (LANES, wide), 1) // CELL
    ).astype(jnp.float32)
    spread[...] = TIME_STEP * jnp.dot(
        spread_in[...], repeat, precision=HIGHEST, preferred_element_type=jnp.float32
    )

    def forward(k, first, final, carry):
        source = state.at[k]
        target = state.at[k + 1]

        def row(x, h, tile, c, a, a2, g_before, mass, count):
            c_next = get(source, x + 1)
            if first:
                vx = [v * (TIME_STEP / 6.0) for v in get(ux, x)]
                vy = [v * (TIME_STEP / 6.0) for v in get(uy, x)]
                put(ux, vx, x)
                put(uy, vy, x)
                well = get(wells, x)
                d = []
                for i in range(pieces):
                    rate = spread[pl.ds(tile * planes, planes), pl.ds(h * cols + i * LANES, LANES)]
                    d.append(KEEP - rate * well[i].astype(jnp.float32))
                put(decay, d, x)
            else:
                vx = get(ux, x)
                vy = get(uy, x)
                d = get(decay, x)
            z = vertical(c, get(halo, k % 2, x))
            c6 = [6.0 * v for v in c]
            b = [n - v for n, v in zip(c_next, c)]
            b2 = [v * v + 0.5 * EPS_LIMIT for v in b]
            flux = []
            out_a, out_b = [], []
            for i in range(pieces):
                w, rs, rq = limiter(a[i], b[i], a2[i] + b2[i])
                t = a[i] + (b[i] + b[i])
                if not first:
                    da, db = slopes(a[i], b[i], t, rs, rq, vx[i] * w)
                    out_a.append(da)
                    out_b.append(db)
                flux.append(vx[i] * (c6[i] + w * t) - DT_FLAT * b[i])
            if not first:
                put(coef, out_a, k - 1, 0, x)
                put(coef, out_b, k - 1, 1, x)
            c_ahead = ahead(c)
            e = [n - v for n, v in zip(c_ahead, c)]
            f = behind(e, c[0])
            side = []
            out_a, out_b = [], []
            for i in range(pieces):
                w, rs, rq = limiter(f[i], e[i], (f[i] * f[i] + e[i] * e[i]) + EPS_LIMIT)
                t = f[i] + (e[i] + e[i])
                if not first:
                    da, db = slopes(f[i], e[i], t, rs, rq, vy[i] * w)
                    out_a.append(da)
                    out_b.append(db)
                side.append(vy[i] * (c6[i] + w * t) - DT_FLAT * e[i])
            if not first:
                put(coef, out_a, k - 1, 2, x)
                put(coef, out_b, k - 1, 3, x)
            side_before = behind(side, -DT_FLAT * c[0])
            new = []
            for i in range(pieces):
                moved = (flux[i] - g_before[i]) + (side[i] - side_before[i])
                new.append((c[i] * d[i] + DT_VERT * z[i]) - moved)
            put(target, new, x)
            if final:
                watch = [m.astype(jnp.float32) for m in get(monitors, x)]
                seed = [m * v for m, v in zip(watch, new)]
                put(lam, seed, 0, x)
                mass = [m + s * v for m, s, v in zip(mass, seed, new)]
                count = [m + s for m, s in zip(count, watch)]
            return c_next, b, b2, flux, mass, count

        def chunk_step(chunk, carry):
            if first:
                ahead_chunk = jnp.minimum(chunk + 1, CHUNKS - 1)

                @pl.when(chunk + 1 < CHUNKS)
                def _():
                    loaded(0, ahead_chunk)

                for which in range(1, 4):
                    loaded(which, chunk)
            if final:
                loaded(4, chunk)
            arrived(k, chunk)

            def group_step(g, carry):
                tile = chunk * groups + g
                for r in range(group):
                    carry = row(tile * group + r, r // CELL, tile, *carry)
                return carry

            carry = lax.fori_loop(0, groups, group_step, carry)
            if final:
                send(lam.at[0], k + 1, chunk)
                span = pl.ds(chunk * size, size)
                for z in range(planes):
                    pltpu.make_async_copy(
                        target.at[span, z, :], fields_hbm.at[0, z, span, :], out_sem.at[chunk]
                    ).start()
            else:
                send(target, k + 1, chunk)
            return carry

        c = get(source, 0)
        a2 = [v * v + 0.5 * EPS_LIMIT for v in c]
        g = [-DT_FLAT * v for v in c]
        none = [zero] * pieces if final else []
        return lax.fori_loop(0, CHUNKS, chunk_step, (c, c, a2, g, none, none))

    loaded(0, 0)
    forward(0, True, False, None)

    def middle(k, carry):
        forward(k, False, False, None)
        return carry

    lax.fori_loop(1, STEPS - 1, middle, 0)
    *_, mass, count = forward(STEPS - 1, False, True, None)
    sums[slab, pl.ds(0, planes), :] = functools.reduce(jnp.add, mass)
    sums[slab, pl.ds(planes, planes), :] = functools.reduce(jnp.add, count)
    sum_copies = everyone("slab", slab, slab_count, sums, sum_send, sum_recv)
    for copy in sum_copies:
        copy.start()

    def backward(k, begin, final):
        e = 2 * STEPS - 1 - k
        slot = (STEPS - 1 - k) % 2
        source = lam.at[slot]
        target = lam.at[1 - slot]

        def row(x, c, n, mu, am, bm_before):
            n2 = get(source, x + 2)
            mu_next = [p - q for p, q in zip(n2, n)]
            am_next = [p * q for p, q in zip(get(coef, k - 1, 0, x + 1), mu_next)]
            bm = [p * q for p, q in zip(get(coef, k - 1, 1, x), mu)]
            side = [p - q for p, q in zip(ahead(c), c)]
            sa = [p * q for p, q in zip(get(coef, k - 1, 2, x), side)]
            sb = [p * q for p, q in zip(get(coef, k - 1, 3, x), side)]
            sa_next = ahead(sa)
            sb_before = behind(sb, -DT_FLAT * c[0])
            vx = get(ux, x)
            vy = get(uy, x)
            d = get(decay, x)
            z = vertical(c, get(halo, e % 2, x))
            past = get(state, k, x)
            kept = [p * q for p, q in zip(past, c)]
            if not begin:
                kept = [p + q for p, q in zip(kept, get(grad, x))]
            new = []
            for i in range(pieces):
                pull = 6.0 * (vx[i] * mu[i] + vy[i] * side[i])
                pull += (am[i] - am_next[i]) + (bm_before[i] - bm[i])
                pull += (sa[i] - sa_next[i]) + (sb_before[i] - sb[i])
                new.append((c[i] * d[i] + DT_VERT * z[i]) + pull)
            if not final:
                put(grad, kept, x)
                put(target, new, x)
            return kept, new, (n, n2, mu_next, am_next, bm)

        def chunk_step(chunk, carry):
            arrived(e, chunk)
            if not final and not begin:
                sent(target, e - 1, chunk)

            def group_step(g, carry):
                tile = chunk * groups + g
                part = None
                for r in range(group):
                    x = tile * group + r
                    kept, new, carry = row(x, *carry)
                    if final:
                        past = get(state, 0, x)
                        well = get(wells, x)
                        term = [
                            (p + q * s) * w.astype(jnp.float32)
                            for p, q, s, w in zip(kept, past, new, well)
                        ]
                        part = term if r % CELL == 0 else [p + q for p, q in zip(part, term)]
                        if r % CELL == CELL - 1:
                            for i in range(pieces):
                                at = (r // CELL) * cols + i * LANES
                                spread[pl.ds(tile * planes, planes), pl.ds(at, LANES)] = part[i]
                return carry

            carry = lax.fori_loop(0, groups, group_step, carry)
            if not final:
                send(target, e + 1, chunk)
            return carry

        c = get(source, 0)
        n = get(source, 1)
        mu = [p - q for p, q in zip(n, c)]
        am = [p * q for p, q in zip(get(coef, k - 1, 0, 0), mu)]
        bm = [-DT_FLAT * p for p in c]
        lax.fori_loop(0, CHUNKS, chunk_step, (c, n, mu, am, bm))

    for k in range(STEPS - 1, 0, -1):
        backward(k, k == STEPS - 1, k == 1)

    narrow = (
        lax.broadcasted_iota(jnp.int32, (wide, LANES), 0) // CELL
        == lax.broadcasted_iota(jnp.int32, (wide, LANES), 1)
    ).astype(jnp.float32)
    flat = jnp.dot(spread[...], narrow, precision=HIGHEST, preferred_element_type=jnp.float32)
    short = tiles * coarse_planes
    fold = (
        lax.broadcasted_iota(jnp.int32, (short, tiles * planes), 0)
        == lax.broadcasted_iota(jnp.int32, (short, tiles * planes), 1) // CELL
    ).astype(jnp.float32)
    shares[...] = jnp.dot(fold, flat, precision=HIGHEST, preferred_element_type=jnp.float32)

    for copy in sum_copies:
        copy.wait()
    both = sums[0]
    for s in range(1, slab_count):
        both = both + sums[s]
    mass = jnp.full((8, LANES), jnp.sum(both[:planes]), jnp.float32)
    count = jnp.full((8, LANES), jnp.sum(both[planes:]), jnp.float32)
    count = jnp.maximum(count, 1.0)
    scaled = (mass / count - threshold[0]) / SOFT_WIDTH
    level_scale = (1.0 - BETA_LEVEL) * scen_count
    decline = jnp.exp(-jnp.abs(scaled))
    weight = jnp.where(scaled >= 0.0, 1.0, decline) / (1.0 + decline) / level_scale
    soft = SOFT_WIDTH * (jnp.maximum(scaled, 0.0) + jnp.log1p(decline)) / level_scale
    coarse_cells = planes * slab_count * rows * cols / float(CELL**3)
    factor = (-TIME_STEP * 2.0 * coarse_cells) * weight / count
    pulls[scen, pl.ds(0, short), :] = shares[...] * factor[0:1]
    pulls[scen, pl.ds(short, 8), :] = soft
    pull_copies = everyone("scen", scen, scen_count, pulls, pull_send, pull_recv)
    for copy in pull_copies:
        copy.start()

    def drain(chunk, carry):
        for e in range(STEPS):
            sent(state.at[e], e, chunk)
        sent(lam.at[1], 2 * STEPS - 3, chunk)
        sent(lam.at[0], 2 * STEPS - 2, chunk)
        target = state.at[STEPS, pl.ds(chunk * size, size)]
        pltpu.make_async_copy(target, target, out_sem.at[chunk]).wait()
        return carry

    lax.fori_loop(0, CHUNKS, drain, 0)

    for copy in pull_copies:
        copy.wait()
    all_pulls = pulls[0]
    for s in range(1, scen_count):
        all_pulls = all_pulls + pulls[s]
    totals[...] = all_pulls
    cvar[0] = threshold[0] + jnp.max(all_pulls[short:])
    for k in range(tiles):
        span = pl.ds(k * LANES, LANES)
        value = cons[:, span] - totals[pl.ds(k * coarse_planes, coarse_planes), :]
        consensus_next[:, span] = value
        multiplier_next[0, :, span] = (multiplier[0, :, span] + control[0, :, span]) - value


def on_device(start, flow_east, flow_north, wells, monitors, control, multiplier, threshold):
    scen_count = lax.axis_size("scen")
    slab_count = lax.axis_size("slab")
    _, planes, rows, cols = start.shape
    _, coarse_planes, coarse = control.shape
    per_lane = LANES // (cols // CELL)
    tiles = rows // (CELL * per_lane)
    short = tiles * coarse_planes
    f32 = jnp.float32
    dma = pltpu.SemaphoreType.DMA
    vmem = pltpu.VMEM
    exchanges = 2 * STEPS - 1
    anywhere = pl.BlockSpec(memory_space=pl.ANY)
    near = pl.BlockSpec(memory_space=pltpu.VMEM)
    scalar = pl.BlockSpec(memory_space=pltpu.SMEM)
    return pl.pallas_call(
        functools.partial(kernel, scen_count, slab_count),
        out_shape=(
            jax.ShapeDtypeStruct(start.shape, f32),
            jax.ShapeDtypeStruct((coarse_planes, coarse), f32),
            jax.ShapeDtypeStruct(control.shape, f32),
            jax.ShapeDtypeStruct((1,), f32),
        ),
        in_specs=[anywhere] * 5 + [near, near, scalar],
        out_specs=(anywhere, near, near, scalar),
        scratch_shapes=[
            vmem((STEPS + 1, rows + 1, planes, cols), f32),
            vmem((2, rows + 2, planes, cols), f32),
            vmem((rows, planes, cols), f32),
            vmem((rows, planes, cols), f32),
            vmem((rows, planes, cols), f32),
            vmem((rows, planes, cols), jnp.int32),
            vmem((rows, planes, cols), jnp.int32),
            vmem((rows, planes, cols), f32),
            vmem((STEPS - 1, 4, rows + 1, planes, cols), f32),
            vmem((2, rows, planes, cols), f32),
            vmem((tiles * planes, LANES), f32),
            vmem((tiles * planes, per_lane * cols), f32),
            vmem((scen_count, coarse_planes, coarse), f32),
            vmem((coarse_planes, coarse), f32),
            vmem((short, LANES), f32),
            vmem((slab_count, 2 * planes, LANES), f32),
            vmem((scen_count, short + 8, LANES), f32),
            vmem((short + 8, LANES), f32),
            dma((5, CHUNKS)),
            dma((CHUNKS,)),
            dma((exchanges, 2, CHUNKS)),
            dma((exchanges, 2, CHUNKS)),
            dma((scen_count - 1,)),
            dma((scen_count - 1,)),
            dma((slab_count - 1,)),
            dma((slab_count - 1,)),
            dma((scen_count - 1,)),
            dma((scen_count - 1,)),
        ],
        compiler_params=pltpu.CompilerParams(
            collective_id=0, has_side_effects=True, vmem_limit_bytes=62 * 1024 * 1024
        ),
        name="window",
    )(start, flow_east, flow_north, wells, monitors, control, multiplier, threshold)


def solution(mesh):
    placed = (
        P("scen", "slab", None, None),
        P("scen", "slab", None, None),
        P("scen", "slab", None, None),
        P("slab", None, None),
        P("slab", None, None),
        P("scen", "slab", None),
        P("scen", "slab", None),
        P(),
    )
    return jax.shard_map(
        on_device,
        mesh=mesh,
        in_specs=placed,
        out_specs=(P("scen", "slab", None, None), P("slab", None), P("scen", "slab", None), P()),
        check_vma=False,
    )
```

time: 431 us -> 87.8 us (0.20); the launches traced: 423 us -> 87.5 us
  other arithmetic: 180 us -> 0 us
  local copies, waits for them, and re-layouts: 152 us -> 4.29 us
  Pallas kernels: 0 us -> 80.1 us
  blocking collectives: 50.6 us -> 0 us
  starting transfers between devices: 34.7 us -> 0 us
    reshape x2 -> x0, local copies, waits for them, and re-layouts: 127 us -> none  [the longest x1 71.4 us: restrict(): fine.reshape(plane_count // 4, 4, row_count // 4, 4, column_count // 4, 4)]
    mul x9 -> x0, other arithmetic: 82.5 us -> none  [the longest x3 37.5 us: horizontal(): return -advect + DIFF_FLAT * spread - rate * field]
    pallas_call x0 -> x1, Pallas kernels: none -> 80.1 us  [on_device(): pl.pallas_call(functools.partial(kernel, scen_count, slab_count), out_sha...]
    psum x3 -> x0, blocking collectives: 50.6 us -> none  [the longest x1 17.7 us: on_device(): lax.psum(jnp.sum(control + multiplier, axis=0), 'scen') / scen_count]
    ppermute x14 -> x0, starting transfers between devices: 34.7 us -> none  [the longest x7 25.7 us: with_halo(): lax.ppermute(tail, axis, [(i, (i + 1) % count) for i in range(ends)])]
    add_any x3 -> x0, other arithmetic: 26.7 us -> none  [divergence(): product = backward * forward]
    reduce_sum x2 -> x0, other arithmetic: 25.8 us -> none  [the longest x1 20.8 us: restrict(): fine.reshape(plane_count // 4, 4, row_count // 4, 4, column_count // 4, 4)]
    neg x3 -> x0, other arithmetic: 25.5 us -> none  [divergence(): backward = field - lower_cells]
  transfers between devices with their start and end apart: 14 -> 0, of which waited for: 0 -> 0; matrix products, arithmetic and copies ran while one was open for 30% -> 0% of each run, Pallas kernels for 0% -> 0%
where the time goes in v1:
time: 87.8 us; the launch traced here: 87.5 us
  Pallas kernels  80.1 us (91%)
  local copies, waits for them, and re-layouts  4.29 us (5%)
  between operations  3.11 us (4%)
    pallas_call x1, Pallas kernels, on_device(): pl.pallas_call(functools.partial(kernel, scen_count, slab_count), out_sha...  80.1 us
    unnamed x7, local copies, waits for them, and re-layouts  4.29 us

profile of v1, /device:TPU:0, one launch (start us, length us, event | category | flops | bytes accessed | tf_op | source)
XLA Modules:
  0.0 87.5 jit_solution(8265144332927176795)
XLA Ops:
  1.3 80.1 %window.1 = (f32[1,8,256,256]{3,2,1,0:T(8,128)}, f32[2,4096]{1,0:T(2,128)}, f32[1,2,4096]{2,1,0:T(2,128)}, f32[1]{0:T(128)}) custom-call(f32[1,8,256,256]{3,2,1,0:T(8,128)} %start_hbm.1, f32[1,8,256,256]{3,2,1,0:T(8,128)} %east_hbm.1, f32[1,8,256,256]{3,2,1,0:T(8,128)} %north_hbm.1, s32[8,256,256]{2,1,0:T(8,128)} %wells_hbm.1, s32[8,256,256]{2,1,0:T(8,128)} %monitors_hbm.1, ...), custom_call_target="tpu_custom_call" | custom-call | tf_op jit(solution)/shard_map/window/pallas_call | solution.py:569
  81.4 0.0 copy-start.1
  81.4 0.0 copy-start
  81.4 3.1 %copy.17 = f32[1,8,256,256]{3,2,1,0:T(8,128)} copy(f32[1,8,256,256]{3,2,1,0:T(8,128)} %get-tuple-element.8) | data formatting | bytes 4194304
  84.5 0.0 copy-done.1
  84.5 0.6 copy.18
  85.1 0.0 copy-done
  85.1 0.6 copy.19
Async XLA Ops:
  81.4 3.1 %copy-start.1 = (f32[2,4096]{1,0:T(2,128)S(1)}, f32[2,4096]{1,0:T(2,128)}, u32[]{:S(2)}) copy-start(f32[2,4096]{1,0:T(2,128)} %get-tuple-element.9) | copy-start | bytes 98308
  81.4 3.7 %copy-start = (f32[1,2,4096]{2,1,0:T(2,128)S(1)}, f32[1,2,4096]{2,1,0:T(2,128)}, u32[]{:S(2)}) copy-start(f32[1,2,4096]{2,1,0:T(2,128)} %get-tuple-element.10) | copy-start | bytes 98308

commit v2 on v1

--- a/solution.py
+++ b/solution.py
@@ -17,7 +17,7 @@
 
 LANES = 128
 CELL = 4
-CHUNKS = 4
+CHUNKS = 2
 
 DT_FLAT = TIME_STEP * DIFF_FLAT
 DT_VERT = TIME_STEP * DIFF_VERTICAL
@@ -337,7 +337,7 @@
                 put(coef, out_b, k - 1, 1, x)
             c_ahead = ahead(c)
             e = [n - v for n, v in zip(c_ahead, c)]
-            f = behind(e, c[0])
+            f = [v - n for v, n in zip(c, behind(c, zero))]
             side = []
             out_a, out_b = [], []
             for i in range(pieces):
@@ -385,7 +385,7 @@
                     carry = row(tile * group + r, r // CELL, tile, *carry)
                 return carry
 
-            carry = lax.fori_loop(0, groups, group_step, carry)
+            carry = lax.fori_loop(0, groups, group_step, carry, unroll=2)
             if final:
                 send(lam.at[0], k + 1, chunk)
                 span = pl.ds(chunk * size, size)
@@ -478,7 +478,7 @@
                                 spread[pl.ds(tile * planes, planes), pl.ds(at, LANES)] = part[i]
                 return carry
 
-            carry = lax.fori_loop(0, groups, group_step, carry)
+            carry = lax.fori_loop(0, groups, group_step, carry, unroll=2)
             if not final:
                 send(target, e + 1, chunk)
             return carry

time: 87.8 us -> 71.6 us (0.82); the launches traced: 87.5 us -> 70.3 us
  Pallas kernels: 80.1 us -> 62.9 us
    pallas_call x1, Pallas kernels: 80.1 us -> 62.9 us  [on_device(): pl.pallas_call(functools.partial(kernel, scen_count, slab_count), out_sha...]
where the time goes in v2:
time: 71.6 us; the launch traced here: 70.3 us
  Pallas kernels  62.9 us (88%)
  local copies, waits for them, and re-layouts  4.29 us (6%)
  between operations  3.11 us (4%)
    pallas_call x1, Pallas kernels, on_device(): pl.pallas_call(functools.partial(kernel, scen_count, slab_count), out_sha...  62.9 us
    unnamed x7, local copies, waits for them, and re-layouts  4.29 us

profile of v2, /device:TPU:0, one launch (start us, length us, event | category | flops | bytes accessed | tf_op | source)
XLA Modules:
  0.0 70.3 jit_solution(18421454344869187612)
XLA Ops:
  1.3 62.9 %window.1 = (f32[1,8,256,256]{3,2,1,0:T(8,128)}, f32[2,4096]{1,0:T(2,128)}, f32[1,2,4096]{2,1,0:T(2,128)}, f32[1]{0:T(128)}) custom-call(f32[1,8,256,256]{3,2,1,0:T(8,128)} %start_hbm.1, f32[1,8,256,256]{3,2,1,0:T(8,128)} %east_hbm.1, f32[1,8,256,256]{3,2,1,0:T(8,128)} %north_hbm.1, s32[8,256,256]{2,1,0:T(8,128)} %wells_hbm.1, s32[8,256,256]{2,1,0:T(8,128)} %monitors_hbm.1, ...), custom_call_target="tpu_custom_call" | custom-call | tf_op jit(solution)/shard_map/window/pallas_call | solution.py:569
  64.2 0.0 copy-start.1
  64.2 0.0 copy-start
  64.2 3.1 %copy.17 = f32[1,8,256,256]{3,2,1,0:T(8,128)} copy(f32[1,8,256,256]{3,2,1,0:T(8,128)} %get-tuple-element.8) | data formatting | bytes 4194304
  67.2 0.0 copy-done.1
  67.2 0.6 copy.18
  67.9 0.0 copy-done
  67.9 0.6 copy.19
Async XLA Ops:
  64.2 3.1 %copy-start.1 = (f32[2,4096]{1,0:T(2,128)S(1)}, f32[2,4096]{1,0:T(2,128)}, u32[]{:S(2)}) copy-start(f32[2,4096]{1,0:T(2,128)} %get-tuple-element.9) | copy-start | bytes 98308
  64.2 3.7 %copy-start = (f32[1,2,4096]{2,1,0:T(2,128)S(1)}, f32[1,2,4096]{2,1,0:T(2,128)}, u32[]{:S(2)}) copy-start(f32[1,2,4096]{2,1,0:T(2,128)} %get-tuple-element.10) | copy-start | bytes 98308
